TPU v7x, 128 devices: a whole 4x4x4 slice. The times are simulated.
128 devices in a mesh: section: 2 (over core), expert: 16 (over z, y), head: 4 (over x).
Axes of the slice: x: 4, y: 4, z: 4, core: 2. Of those that a mesh axis runs over, the one named last changes fastest.
Arguments:
- inputs: bfloat16 [2, 2048, 768], P(None, 'expert'), may hold values from -6 to 6
- cotangent: bfloat16 [2, 2048, 768], P(None, 'expert'), may hold values from -6 to 6
- routes: int32 [2, 2, 2048, 2], P('section', None, 'expert'), may hold values from 0 to 31, all different within a row; in each aligned block of 128 rows (0 to 127, 128 to 255, ..., all dimensions but the last counted through in order) at most 12 rows name the same one
- attend_gain: bfloat16 [2, 768], P('section'), may hold values from 0.099609375 to 1.8984375
- query_key_value: bfloat16 [2, 3, 768, 768], P('section', None, None, 'head'), may hold values from -0.21875 to 0.21875
- attend_out: bfloat16 [2, 768, 768], P('section', 'head'), may hold values from -1.75 to 1.75
- position_bias: bfloat16 [2, 12, 32], P('section', 'head'), may hold values from -4 to 4
- mixture_gain: bfloat16 [2, 768], P('section'), may hold values from 0.099609375 to 1.8984375
- router: bfloat16 [2, 768, 32], P('section'), may hold values from -0.15625 to 0.15625
- expert_up: bfloat16 [2, 32, 768, 3072], P('section', 'expert', None, 'head'), may hold values from -0.21875 to 0.21875
- expert_down: bfloat16 [2, 32, 3072, 768], P('section', 'expert', 'head'), may hold values from -0.109375 to 0.109375
Outputs:
- section_output: bfloat16 [2, 2, 2048, 768], P('section', None, 'expert')
- input_grad: float32 [2, 2, 2048, 768], P('section', None, 'expert')
- grad_attend_gain: float32 [2, 768], P('section')
- grad_query_key_value: float32 [2, 3, 768, 768], P('section', None, None, 'head')
- grad_attend_out: float32 [2, 768, 768], P('section', 'head')
- grad_position_bias: float32 [2, 12, 32], P('section', 'head')
- grad_mixture_gain: float32 [2, 768], P('section')
- grad_router: float32 [2, 768, 32], P('section')
- grad_expert_up: float32 [2, 32, 768, 3072], P('section', 'expert', None, 'head')
- grad_expert_down: float32 [2, 32, 3072, 768], P('section', 'expert', 'head')
Inputs may be any that keep to these rules, and one draw needn't show every extreme that they name: `routes`: each token names two different experts. Among the 128 tokens of one sequence (one section, micro-batch and index of expert), no expert is named more than 12 times over both slots, and in every draw some expert is named exactly 12 times by some sequence.
All inputs are finite; a program needn't handle non-finite values.
Results may differ from a plain program's by a relative error of at most 0.028.
Values may be sent and summed in bfloat16 or wider, within the bound.
No kernel may reach another device: no remote copies, remote signals or barrier semaphores. Data moves between devices by JAX's collectives and lax.ppermute only.
A program may use at most 128 MiB of HBM per device.

v0:
```python
import jax
import jax.numpy as jnp
from jax import lax
from jax.sharding import PartitionSpec as P

HEAD_DIM = 64
EPS = 1e-06
NEG = -1e30


def passed_along(array, axis, by):
    length = lax.axis_size(axis)
    pairs = [(i, i + by) for i in range(length) if 0 <= i + by < length]
    return lax.ppermute(array, axis, pairs)


def norm_scale(values):
    return lax.rsqrt(jnp.mean(values * values, axis=-1, keepdims=True) + EPS)


def norm_back(grad_normed, values, scale, gain):
    unit = values * scale
    grad_gain = jnp.sum(grad_normed * unit, axis=0)
    grad_unit = grad_normed * gain
    grad_values = scale * (grad_unit - unit * jnp.mean(grad_unit * unit, axis=-1, keepdims=True))
    return (grad_values, grad_gain)


def position_tables(length, buckets):
    rows = lax.broadcasted_iota(jnp.int32, (length, length), 0)
    cols = lax.broadcasted_iota(jnp.int32, (length, length), 1)
    offset = rows - cols
    levels = lax.broadcasted_iota(jnp.int32, (buckets, length, length), 0)
    onehot = (jnp.clip(offset, 0, buckets - 1)[None] == levels).astype(jnp.bfloat16)
    return (offset >= 0, onehot)


def slot_targets(route_tile, experts, capacity):
    flat = route_tile.reshape(-1)
    levels = lax.broadcasted_iota(jnp.int32, (flat.shape[0], experts), 1)
    onehot = (flat[:, None] == levels).astype(jnp.int32)
    place = jnp.sum((jnp.cumsum(onehot, axis=0) - 1) * onehot, axis=1)
    return flat * capacity + place


def attend_scores(heads, table, causal, onehot):
    bias = jnp.einsum("bst,hb->hst", onehot, table, preferred_element_type=jnp.float32)
    scores = jnp.einsum("shd,thd->hst", heads[0], heads[1], preferred_element_type=jnp.float32)
    scores = scores * HEAD_DIM ** (-0.5) + bias
    return jnp.where(causal[None], scores, NEG)


def attend_forward(normed, proj_weight, out_weight, table, causal, onehot):
    length = normed.shape[0]
    local_heads = table.shape[0]
    projected = jnp.einsum(
        "sd,kde->kse", normed, proj_weight, preferred_element_type=jnp.float32
    ).astype(jnp.bfloat16)
    heads = projected.reshape(3, length, local_heads, HEAD_DIM)
    scores = attend_scores(heads, table, causal, onehot)
    top = jnp.max(scores, axis=-1, keepdims=True)
    weights = jnp.exp(scores - top)
    total = jnp.sum(weights, axis=-1, keepdims=True)
    probs = (weights / total).astype(jnp.bfloat16)
    mixed = jnp.einsum("hst,thd->shd", probs, heads[2], preferred_element_type=jnp.float32)
    mixed = mixed.reshape(length, local_heads * HEAD_DIM).astype(jnp.bfloat16)
    partial_out = jnp.dot(mixed, out_weight, preferred_element_type=jnp.float32)
    return (partial_out, (projected, mixed, top + jnp.log(total)))


def attend_backward(grad_attn, normed, proj_weight, out_weight, table, causal, onehot, saved_attn):
    projected, mixed, log_total = saved_attn
    length = normed.shape[0]
    local_heads = table.shape[0]
    heads = projected.reshape(3, length, local_heads, HEAD_DIM)
    grad_out_weight = jnp.einsum("se,sd->ed", mixed, grad_attn, preferred_element_type=jnp.float32)
    grad_mixed = jnp.einsum("sd,ed->se", grad_attn, out_weight, preferred_element_type=jnp.float32)
    grad_mixed = grad_mixed.astype(jnp.bfloat16).reshape(length, local_heads, HEAD_DIM)
    probs = jnp.exp(attend_scores(heads, table, causal, onehot) - log_total)
    grad_probs = jnp.einsum(
        "shd,thd->hst", grad_mixed, heads[2], preferred_element_type=jnp.float32
    )
    delta = jnp.sum(probs * grad_probs, axis=-1, keepdims=True)
    grad_scores = (probs * (grad_probs - delta)).astype(jnp.bfloat16)
    grad_table = jnp.einsum("bst,hst->hb", onehot, grad_scores, preferred_element_type=jnp.float32)
    factor = HEAD_DIM ** (-0.5)
    grad_query = (
        jnp.einsum("hst,thd->shd", grad_scores, heads[1], preferred_element_type=jnp.float32)
        * factor
    )
    grad_key = (
        jnp.einsum("hst,shd->thd", grad_scores, heads[0], preferred_element_type=jnp.float32)
        * factor
    )
    grad_value = jnp.einsum(
        "hst,shd->thd", probs.astype(jnp.bfloat16), grad_mixed, preferred_element_type=jnp.float32
    )
    grad_projected = (
        jnp.stack([grad_query, grad_key, grad_value])
        .reshape(3, length, local_heads * HEAD_DIM)
        .astype(jnp.bfloat16)
    )
    grad_proj_weight = jnp.einsum(
        "sd,kse->kde", normed, grad_projected, preferred_element_type=jnp.float32
    )
    grad_normed = jnp.einsum(
        "kse,kde->sd", grad_projected, proj_weight, preferred_element_type=jnp.float32
    )
    return (grad_normed, grad_proj_weight, grad_out_weight, grad_table)


def raise_hidden(arrived, up_weight):
    pre_act = jnp.einsum("erd,edf->erf", arrived, up_weight, preferred_element_type=jnp.float32)
    return (pre_act, jax.nn.gelu(pre_act).astype(jnp.bfloat16))


def gate_forward(logits, route_tile, experts):
    levels = lax.broadcasted_iota(jnp.int32, route_tile.shape + (experts,), 2)
    pick = (route_tile[:, :, None] == levels).astype(jnp.float32)
    chosen = jnp.sum(logits[:, None, :] * pick, axis=-1)
    top = jnp.max(chosen, axis=-1, keepdims=True)
    weights = jnp.exp(chosen - top)
    return (weights / jnp.sum(weights, axis=-1, keepdims=True), pick)


def layer_forward(layer_in, route_tile, params, tables):
    gain_a, proj_weight, out_weight, table, gain_m, router_weight, up_weight, down_weight = params
    causal, onehot = tables
    values = layer_in.astype(jnp.float32)
    length, width = values.shape
    experts = router_weight.shape[1]
    local_experts = up_weight.shape[0]
    capacity = 3 * length // experts
    scale_a = norm_scale(values)
    normed_a = (values * scale_a * gain_a).astype(jnp.bfloat16)
    partial_attn, saved_attn = attend_forward(
        normed_a, proj_weight, out_weight, table, causal, onehot
    )
    attended = lax.psum(partial_attn, "head")
    middle = values + attended
    scale_m = norm_scale(middle)
    normed_m = (middle * scale_m * gain_m).astype(jnp.bfloat16)
    logits = jnp.dot(normed_m, router_weight, preferred_element_type=jnp.float32)
    gates, pick = gate_forward(logits, route_tile, experts)
    target = slot_targets(route_tile, experts, capacity)
    buffer = (
        jnp.zeros((experts * capacity, width), jnp.bfloat16)
        .at[target]
        .set(jnp.repeat(normed_m, 2, axis=0))
    )
    arrived = lax.all_to_all(
        buffer.reshape(experts, 1, capacity, width),
        "expert",
        split_axis=0,
        concat_axis=1,
        tiled=True,
    )
    arrived = arrived.reshape(local_experts, -1, width)
    pre_act, hidden = raise_hidden(arrived, up_weight)
    partial_rows = jnp.einsum(
        "erf,efd->erd", hidden, down_weight, preferred_element_type=jnp.float32
    )
    returned = lax.all_to_all(
        partial_rows.reshape(local_experts, -1, capacity, width).astype(jnp.bfloat16),
        "expert",
        split_axis=1,
        concat_axis=0,
        tiled=True,
    ).astype(jnp.float32)
    slot_part = returned.reshape(experts * capacity, width)[target].reshape(length, 2, width)
    slot_out = lax.psum(slot_part.astype(jnp.bfloat16), "head").astype(jnp.float32)
    layer_out = middle + jnp.sum(gates[:, :, None] * slot_out, axis=1)
    owner_saved = (buffer,)
    saved = (
        values,
        scale_a,
        normed_a,
        saved_attn,
        middle,
        scale_m,
        normed_m,
        gates,
        pick,
        target,
        slot_out,
        owner_saved,
    )
    return (layer_out, saved)


def layer_backward(grad_out, saved, params, tables):
    gain_a, proj_weight, out_weight, table, gain_m, router_weight, up_weight, down_weight = params
    causal, onehot = tables
    (
        values,
        scale_a,
        normed_a,
        saved_attn,
        middle,
        scale_m,
        normed_m,
        gates,
        pick,
        target,
        slot_out,
        owner_saved,
    ) = saved
    length, width = values.shape
    experts = router_weight.shape[1]
    local_experts = up_weight.shape[0]
    capacity = 3 * length // experts
    grad_slots = (gates[:, :, None] * grad_out[:, None, :]).astype(jnp.bfloat16)
    grad_gates = jnp.sum(grad_out[:, None, :] * slot_out, axis=-1)
    grad_buffer = (
        jnp.zeros((experts * capacity, width), jnp.bfloat16)
        .at[target]
        .set(grad_slots.reshape(2 * length, width))
    )
    grad_buffer = grad_buffer.reshape(experts, 1, capacity, width)
    row_buffer = owner_saved[0].reshape(experts, 1, capacity, width)
    grad_arrived, arrived = (
        lax.all_to_all(grad_buffer, "expert", split_axis=0, concat_axis=1, tiled=True),
        lax.all_to_all(row_buffer, "expert", split_axis=0, concat_axis=1, tiled=True),
    )
    arrived = arrived.reshape(local_experts, -1, width)
    pre_act, hidden = raise_hidden(arrived, up_weight)
    grad_arrived = grad_arrived.reshape(local_experts, -1, width)
    grad_hidden = jnp.einsum(
        "erd,efd->erf", grad_arrived, down_weight, preferred_element_type=jnp.float32
    )
    unused, gelu_back = jax.vjp(jax.nn.gelu, pre_act)
    grad_pre = gelu_back(grad_hidden)[0].astype(jnp.bfloat16)
    grad_down = jnp.einsum("erf,erd->efd", hidden, grad_arrived, preferred_element_type=jnp.float32)
    grad_up = jnp.einsum("erd,erf->edf", arrived, grad_pre, preferred_element_type=jnp.float32)
    grad_rows = jnp.einsum("erf,edf->erd", grad_pre, up_weight, preferred_element_type=jnp.float32)
    returned = lax.all_to_all(
        grad_rows.reshape(local_experts, -1, capacity, width).astype(jnp.bfloat16),
        "expert",
        split_axis=1,
        concat_axis=0,
        tiled=True,
    ).astype(jnp.float32)
    grad_slot_rows = returned.reshape(experts * capacity, width)[target].reshape(length, 2, width)
    grad_normed_m = lax.psum(jnp.sum(grad_slot_rows, axis=1).astype(jnp.bfloat16), "head").astype(
        jnp.float32
    )
    grad_chosen = gates * (grad_gates - jnp.sum(gates * grad_gates, axis=-1, keepdims=True))
    grad_logits = jnp.sum(grad_chosen[:, :, None] * pick, axis=1).astype(jnp.bfloat16)
    grad_router = jnp.einsum("sd,se->de", normed_m, grad_logits, preferred_element_type=jnp.float32)
    grad_normed_m = grad_normed_m + jnp.einsum(
        "se,de->sd", grad_logits, router_weight, preferred_element_type=jnp.float32
    )
    grad_middle, grad_gain_m = norm_back(grad_normed_m, middle, scale_m, gain_m)
    grad_middle = grad_middle + grad_out
    grad_normed_a, grad_proj_weight, grad_out_weight, grad_table = attend_backward(
        grad_middle.astype(jnp.bfloat16),
        normed_a,
        proj_weight,
        out_weight,
        table,
        causal,
        onehot,
        saved_attn,
    )
    grad_normed_a = lax.psum(grad_normed_a.astype(jnp.bfloat16), "head").astype(jnp.float32)
    grad_values, grad_gain_a = norm_back(grad_normed_a, values, scale_a, gain_a)
    shared = (grad_gain_a, grad_proj_weight, grad_out_weight, grad_table, grad_gain_m, grad_router)
    return (grad_values + grad_middle, shared, (grad_up, grad_down))


def on_device(
    inputs,
    cotangent,
    routes,
    attend_gain,
    query_key_value,
    attend_out,
    position_bias,
    mixture_gain,
    router,
    expert_up,
    expert_down,
):
    micro = inputs.shape[0]
    length = inputs.shape[1]
    params = (
        attend_gain[0].astype(jnp.float32),
        query_key_value[0],
        attend_out[0],
        position_bias[0],
        mixture_gain[0].astype(jnp.float32),
        router[0],
        expert_up[0],
        expert_down[0],
    )
    tables = position_tables(length, position_bias.shape[2])
    first = lax.axis_index("section") == 0
    received = jnp.zeros((length, inputs.shape[2]), jnp.bfloat16)
    outputs = []
    caches = []
    for tick in range(micro + 1):
        layer_in = jnp.where(first, inputs[min(tick, micro - 1)], received)
        route_tile = jnp.where(first, routes[0, min(tick, micro - 1)], routes[0, max(tick - 1, 0)])
        layer_out, saved = layer_forward(layer_in, route_tile, params, tables)
        layer_low = layer_out.astype(jnp.bfloat16)
        outputs.append(layer_low)
        caches.append(saved)
        if tick < micro:
            received = passed_along(layer_low, "section", 1)
    section_output = jnp.stack(
        [jnp.where(first, outputs[index], outputs[index + 1]) for index in range(micro)]
    )[None]
    grad_received = jnp.zeros_like(received)
    shared_total = None
    owned_total = None
    grad_list = []
    for tick in range(micro + 1):
        late = cotangent[min(tick, micro - 1)].astype(jnp.float32)
        if tick == micro:
            late = jnp.zeros_like(late)
        grad_out = jnp.where(first, grad_received.astype(jnp.float32), late)
        saved = jax.tree.map(
            lambda early, later: jnp.where(first, early, later),
            caches[max(tick - 1, 0)],
            caches[min(tick + 1, micro)],
        )
        grad_in, shared, owned = layer_backward(grad_out, saved, params, tables)
        if shared_total is None:
            shared_total = shared
            owned_total = owned
        else:
            shared_total = jax.tree.map(lambda total, extra: total + extra, shared_total, shared)
            owned_total = jax.tree.map(lambda total, extra: total + extra, owned_total, owned)
        grad_list.append(grad_in)
        if tick < micro:
            grad_received = passed_along(grad_in.astype(jnp.bfloat16), "section", -1)
    gain_a, proj_part, out_part, table_part, gain_m, router_part = shared_total
    shared_total = (
        lax.psum(gain_a.astype(jnp.bfloat16), "expert").astype(jnp.float32),
        lax.psum(proj_part.astype(jnp.bfloat16), "expert").astype(jnp.float32),
        lax.psum(out_part.astype(jnp.bfloat16), "expert").astype(jnp.float32),
        lax.psum(table_part.astype(jnp.bfloat16), "expert").astype(jnp.float32),
        lax.psum(gain_m.astype(jnp.bfloat16), "expert").astype(jnp.float32),
        lax.psum(router_part.astype(jnp.bfloat16), "expert").astype(jnp.float32),
    )
    input_grad = jnp.stack(
        [jnp.where(first, grad_list[index + 1], grad_list[index]) for index in range(micro)]
    )[None]
    grad_gain_a, grad_proj, grad_out_weight, grad_table, grad_gain_m, grad_router = shared_total
    grad_up, grad_down = owned_total
    return (
        section_output,
        input_grad,
        grad_gain_a[None],
        grad_proj[None],
        grad_out_weight[None],
        grad_table[None],
        grad_gain_m[None],
        grad_router[None],
        grad_up[None],
        grad_down[None],
    )


def solution(mesh):
    return jax.shard_map(
        on_device,
        mesh=mesh,
        in_specs=(
            P(None, "expert", None),
            P(None, "expert", None),
            P("section", None, "expert", None),
            P("section", None),
            P("section", None, None, "head"),
            P("section", "head", None),
            P("section", "head", None),
            P("section", None),
            P("section", None, None),
            P("section", "expert", None, "head"),
            P("section", "expert", "head", None),
        ),
        out_specs=(
            P("section", None, "expert", None),
            P("section", None, "expert", None),
            P("section", None),
            P("section", None, None, "head"),
            P("section", "head", None),
            P("section", "head", None),
            P("section", None),
            P("section", None, None),
            P("section", "expert", None, "head"),
            P("section", "expert", "head", None),
        ),
        check_vma=False,
    )
```

profile of v0, /device:TPU:0, one launch (start us, length us, event | category | flops | bytes accessed | tf_op | source)
XLA Modules:
  0.0 950.1 jit_solution(12501314368429168360)
XLA Ops:
  22.1 39.1 %all-reduce.16.cloned.1.call-done = f32[128,768]{1,0:T(8,128)} async-done(((f32[128,768]{1,0:T(8,128)}), f32[128,768]{1,0:T(8,128)}) %all-reduce.16.cloned.1.call-update) | async-done | bytes 393232 | tf_op jit(solution)/shard_map/psum | solution.py:139
  68.0 19.2 %all_to_all.189 = bf16[32,1,12,768]{3,2,1,0:T(8,128)(2,1)S(1)} all-to-all(bf16[32,1,12,768]{3,2,1,0:T(8,128)(2,1)} %bitcast.600), channel_id=1, replica_groups=mesh['section'=2,'expert'=16,'head'=4] {'expert'}, dimensions={0} | all-to-all | bytes 1179648 | tf_op jit(solution)/shard_map/all_to_all | solution.py:151
  98.2 10.2 %all-to-all-done.1 = bf16[2,16,12,768]{3,0,2,1:T(2,128)(2,1)S(1)} async-done(((bf16[2,16,12,768]{3,0,2,1:T(2,128)(2,1)}), bf16[2,16,12,768]{3,0,2,1:T(2,128)(2,1)S(1)}, u32[]{:S(2)}, u32[]{:S(2)}) %all-to-all-start.1) | async-done | bytes 589856 | tf_op jit(solution)/shard_map/all_to_all | solution.py:163
  114.5 38.0 %all-reduce.18.cloned.1.call-done = bf16[128,2,768]{2,1,0:T(2,128)(2,1)} async-done(((bf16[128,2,768]{2,1,0:T(2,128)(2,1)}), bf16[128,2,768]{2,1,0:T(2,128)(2,1)}) %all-reduce.18.cloned.1.call-update) | async-done | bytes 393232 | tf_op jit(solution)/shard_map/psum | solution.py:171
  164.4 40.4 %all-reduce.20.cloned.1.call-done = f32[128,768]{1,0:T(8,128)} async-done(((f32[128,768]{1,0:T(8,128)}), f32[128,768]{1,0:T(8,128)}) %all-reduce.20.cloned.1.call-update) | async-done | bytes 393232 | tf_op jit(solution)/shard_map/psum | solution.py:139
  214.6 7.0 all-to-all-start.7
  225.1 8.9 all-to-all-done.7
  244.1 5.9 all-to-all-done.2
  250.1 4.3 all-to-all-start.6
  266.0 6.9 all-to-all-start.3
  284.2 5.0 all-to-all-start.8
  317.0 37.1 %all-reduce.36.cloned.1.call-done = (bf16[128,768]{1,0:T(8,128)(2,1)}, bf16[128,2,768]{2,1,0:T(2,128)(2,1)}) async-done(((bf16[128,768]{1,0:T(8,128)(2,1)}, bf16[128,2,768]{2,1,0:T(2,128)(2,1)}), (bf16[128,768]{1,0:T(8,128)(2,1)}, bf16[128,2,768]{2,1,0:T(2,128)(2,1)})) %all-reduce.36.cloned.1.call-update) | async-done | bytes 589840 | tf_op jit(solution)/shard_map/psum | solution.py:244
  369.2 38.2 %all-reduce.24.cloned.1.call-done = bf16[128,768]{1,0:T(8,128)(2,1)} async-done(((bf16[128,768]{1,0:T(8,128)(2,1)}), bf16[128,768]{1,0:T(8,128)(2,1)}) %all-reduce.24.cloned.1.call-update) | async-done | bytes 196624 | tf_op jit(solution)/shard_map/psum | solution.py:265
  420.9 37.7 %all-reduce.22.cloned.1.call-done = f32[128,768]{1,0:T(8,128)} async-done(((f32[128,768]{1,0:T(8,128)}), f32[128,768]{1,0:T(8,128)}) %all-reduce.22.cloned.1.call-update) | async-done | bytes 393232 | tf_op jit(solution)/shard_map/psum | solution.py:139
  472.0 7.2 all-to-all-start.13
  486.3 5.2 all-to-all-done.13
  491.6 4.5 all-to-all-start.4
  504.0 6.3 all-to-all-done.4
  510.3 4.3 all-to-all-start.10
  520.0 7.7 all-to-all-done.10
  544.7 7.4 all-to-all-start.5
  562.6 4.8 all-to-all-start.11
  595.1 37.2 %all-reduce.34.cloned.1.call-done = (bf16[128,768]{1,0:T(8,128)(2,1)}, bf16[128,2,768]{2,1,0:T(2,128)(2,1)}) async-done(((bf16[128,768]{1,0:T(8,128)(2,1)}, bf16[128,2,768]{2,1,0:T(2,128)(2,1)}), (bf16[128,768]{1,0:T(8,128)(2,1)}, bf16[128,2,768]{2,1,0:T(2,128)(2,1)})) %all-reduce.34.cloned.1.call-update) | async-done | bytes 589840 | tf_op jit(solution)/shard_map/psum | solution.py:244
  649.4 39.0 %all-reduce.26.cloned.1.call-done = bf16[128,768]{1,0:T(8,128)(2,1)} async-done(((bf16[128,768]{1,0:T(8,128)(2,1)}), bf16[128,768]{1,0:T(8,128)(2,1)}) %all-reduce.26.cloned.1.call-update) | async-done | bytes 196624 | tf_op jit(solution)/shard_map/psum | solution.py:265
  707.3 7.2 all-to-all-start.12
  717.3 11.9 %all-to-all-done.12 = bf16[32,1,12,768]{3,2,1,0:T(8,128)(2,1)} async-done(((bf16[32,1,12,768]{3,2,1,0:T(8,128)(2,1)}), bf16[32,1,12,768]{3,2,1,0:T(8,128)(2,1)}, u32[]{:S(2)}, u32[]{:S(2)}) %all-to-all-start.12) | async-done | bytes 589856 | tf_op jit(solution)/shard_map/all_to_all | solution.py:222
  741.2 7.2 add_bitcast_fusion
  762.5 7.3 add_bitcast_fusion.1
  769.7 30.9 %all-reduce.28.cloned.1.call-done = bf16[128,768]{1,0:T(8,128)(2,1)} async-done(((bf16[128,768]{1,0:T(8,128)(2,1)}), bf16[128,768]{1,0:T(8,128)(2,1)}) %all-reduce.28.cloned.1.call-update) | async-done | bytes 196624 | tf_op jit(solution)/shard_map/psum | solution.py:244
  816.8 31.7 %all-reduce.30.cloned.1.call-done = bf16[128,768]{1,0:T(8,128)(2,1)} async-done(((bf16[128,768]{1,0:T(8,128)(2,1)}), bf16[128,768]{1,0:T(8,128)(2,1)}) %all-reduce.30.cloned.1.call-update) | async-done | bytes 196624 | tf_op jit(solution)/shard_map/psum | solution.py:265
  850.9 75.9 %all-reduce = (bf16[1,3,32]{2,1,0:T(4,128)(2,1)}, bf16[1,768]{1,0:T(2,128)(2,1)}, bf16[1,768]{1,0:T(2,128)(2,1)S(1)}, bf16[1,768,32]{1,2,0:T(8,128)(2,1)}) all-reduce(bf16[1,3,32]{2,1,0:T(4,128)(2,1)} %fusion.153, bf16[1,768]{1,0:T(2,128)(2,1)S(1)} %broadcast_in_dim.93, ...), channel_id=1, replica_groups=mesh['section'=2,'expert'=16,'head'=4] {'expert'}, use_global_device_ids=true, to_apply=%region_78.79 | all-reduce | flops 26208 | bytes 104832 | tf_op jit(solution)/shard_map/psum | solution.py:342
  934.2 6.0 all-reduce.32.cloned.1.call-done
  (793 shorter events, 333.5 us)
Async XLA Ops:
  7.2 54.1 %all-reduce.16.cloned.1.call-start = ((), (), s32[]{:S(2)}) async-start(), calls=%async_computation.15 | async-start | bytes 786432 | tf_op jit(solution)/shard_map/psum | solution.py:139
  8.6 149.8 %copy-start.203 = (f32[128]{0:T(128)}, f32[128]{0:T(128)S(1)}, u32[]{:S(2)}) copy-start(f32[128]{0:T(128)S(1)} %fusion.245) | copy-start | bytes 1540
  9.3 149.7 %copy-start.103 = (f32[768]{0:T(1024)}, f32[768]{0:T(1024)S(1)}, u32[]{:S(2)}) copy-start(f32[768]{0:T(1024)S(1)} %convert_reduce_fusion.1) | copy-start | bytes 9220
  20.6 185.8 %copy-start.119 = (f32[768]{0:T(1024)}, f32[768]{0:T(1024)S(1)}, u32[]{:S(2)}) copy-start(f32[768]{0:T(1024)S(1)} %convert_reduce_fusion) | copy-start | bytes 9220
  94.4 14.0 %all-to-all-start.1 = ((bf16[2,16,12,768]{3,0,2,1:T(2,128)(2,1)}), bf16[2,16,12,768]{3,0,2,1:T(2,128)(2,1)S(1)}, u32[]{:S(2)}, u32[]{:S(2)}) async-start(bf16[2,16,12,768]{3,0,2,1:T(2,128)(2,1)} %bitcast.613), calls=%async_computation.1 | async-start | bytes 1179648 | tf_op jit(solution)/shard_map/all_to_all | solution.py:163
  97.9 54.5 %all-reduce.18.cloned.1.call-start = ((), (), s32[]{:S(2)}) async-start(), calls=%async_computation.16 | async-start | bytes 786432 | tf_op jit(solution)/shard_map/psum | solution.py:171
  113.2 91.6 %all-reduce.20.cloned.1.call-start = ((), (), s32[]{:S(2)}) async-start(), calls=%async_computation.17 | async-start | bytes 786432 | tf_op jit(solution)/shard_map/psum | solution.py:139
  155.7 2.5 collective-permute-start
  214.6 19.4 %all-to-all-start.7 = ((bf16[32,1,12,768]{3,2,1,0:T(8,128)(2,1)}), bf16[32,1,12,768]{3,2,1,0:T(8,128)(2,1)}, u32[]{:S(2)}, u32[]{:S(2)}) async-start(bf16[32,1,12,768]{3,2,1,0:T(8,128)(2,1)} %bitcast.598), calls=%async_computation.7 | async-start | bytes 1572864 | tf_op jit(solution)/shard_map/all_to_all | solution.py:223
  234.0 16.1 %all-to-all-start.2 = ((bf16[32,1,12,768]{3,2,1,0:T(8,128)(2,1)}), bf16[32,1,12,768]{3,2,1,0:T(8,128)(2,1)}, u32[]{:S(2)}, u32[]{:S(2)}) async-start(bf16[32,1,12,768]{3,2,1,0:T(8,128)(2,1)} %bitcast.596), calls=%async_computation.2 | async-start | bytes 1572864 | tf_op jit(solution)/shard_map/all_to_all | solution.py:151
  250.1 15.9 %all-to-all-start.6 = ((bf16[32,1,12,768]{3,2,1,0:T(8,128)(2,1)}), bf16[32,1,12,768]{3,2,1,0:T(8,128)(2,1)}, u32[]{:S(2)}, u32[]{:S(2)}) async-start(bf16[32,1,12,768]{3,2,1,0:T(8,128)(2,1)} %bitcast.80), calls=%async_computation.6 | async-start | bytes 1572864 | tf_op jit(solution)/shard_map/all_to_all | solution.py:222
  266.0 17.4 %all-to-all-start.3 = ((bf16[2,16,12,768]{3,0,2,1:T(2,128)(2,1)}), bf16[2,16,12,768]{3,0,2,1:T(2,128)(2,1)S(1)}, u32[]{:S(2)}, u32[]{:S(2)}) async-start(bf16[2,16,12,768]{3,0,2,1:T(2,128)(2,1)} %bitcast.611), calls=%async_computation.3 | async-start | bytes 1179648 | tf_op jit(solution)/shard_map/all_to_all | solution.py:163
  284.2 15.4 %all-to-all-start.8 = ((bf16[2,16,12,768]{3,0,2,1:T(2,128)(2,1)}), bf16[2,16,12,768]{3,0,2,1:T(2,128)(2,1)S(1)}, u32[]{:S(2)}, u32[]{:S(2)}) async-start(bf16[2,16,12,768]{3,0,2,1:T(2,128)(2,1)} %bitcast.88), calls=%async_computation.8 | async-start | bytes 1179648 | tf_op jit(solution)/shard_map/all_to_all | solution.py:236
  289.1 64.9 %all-reduce.36.cloned.1.call-start = ((), (), s32[]{:S(2)}) async-start(), calls=%async_computation.25 | async-start | bytes 1179648 | tf_op jit(solution)/shard_map/psum | solution.py:244
  310.3 97.2 %all-reduce.24.cloned.1.call-start = ((), (), s32[]{:S(2)}) async-start(), calls=%async_computation.19 | async-start | bytes 393216 | tf_op jit(solution)/shard_map/psum | solution.py:265
  365.2 93.4 %all-reduce.22.cloned.1.call-start = ((), (), s32[]{:S(2)}) async-start(), calls=%async_computation.18 | async-start | bytes 786432 | tf_op jit(solution)/shard_map/psum | solution.py:139
  367.3 42.1 %collective-permute-start.1 = (bf16[128,768]{1,0:T(8,128)(2,1)S(1)}, bf16[128,768]{1,0:T(8,128)(2,1)}, u32[]{:S(2)}, u32[]{:S(2)}) collective-permute-start(bf16[128,768]{1,0:T(8,128)(2,1)S(1)} %get-tuple-element.84), channel_id=1, source_target_pairs={{0,64},{1,65},{2,66},{3,67},{4,68},{5,69},{6,70},{7,71},{8,72},{9,... | collective-permute-start | bytes 589832 | tf_op jit(solution)/shard_map/ppermute | solution.py:14
  472.0 19.5 %all-to-all-start.13 = ((bf16[32,1,12,768]{3,2,1,0:T(8,128)(2,1)}), bf16[32,1,12,768]{3,2,1,0:T(8,128)(2,1)}, u32[]{:S(2)}, u32[]{:S(2)}) async-start(bf16[32,1,12,768]{3,2,1,0:T(8,128)(2,1)} %bitcast.129), calls=%async_computation.13 | async-start | bytes 1572864 | tf_op jit(solution)/shard_map/all_to_all | solution.py:223
  481.3 16.1 %collective-permute-start.2 = (bf16[128,768]{1,0:T(8,128)(2,1)}, bf16[128,768]{1,0:T(8,128)(2,1)}, u32[]{:S(2)}, u32[]{:S(2)}) collective-permute-start(bf16[128,768]{1,0:T(8,128)(2,1)} %get-tuple-element.99), channel_id=1, source_target_pairs={{64,0},{65,1},{66,2},{67,3},{68,4},{69,5},{70,6},{71,7},{72,8},{73... | collective-permute-start | bytes 589832 | tf_op jit(solution)/shard_map/ppermute | solution.py:14
  491.6 18.7 %all-to-all-start.4 = ((bf16[32,1,12,768]{3,2,1,0:T(8,128)(2,1)}), bf16[32,1,12,768]{3,2,1,0:T(8,128)(2,1)}, u32[]{:S(2)}, u32[]{:S(2)}) async-start(bf16[32,1,12,768]{3,2,1,0:T(8,128)(2,1)} %bitcast.595), calls=%async_computation.4 | async-start | bytes 1572864 | tf_op jit(solution)/shard_map/all_to_all | solution.py:151
  510.3 17.3 %all-to-all-start.10 = ((bf16[32,1,12,768]{3,2,1,0:T(8,128)(2,1)}), bf16[32,1,12,768]{3,2,1,0:T(8,128)(2,1)}, u32[]{:S(2)}, u32[]{:S(2)}) async-start(bf16[32,1,12,768]{3,2,1,0:T(8,128)(2,1)} %bitcast.594), calls=%async_computation.10 | async-start | bytes 1572864 | tf_op jit(solution)/shard_map/all_to_all | solution.py:223
  527.6 17.1 %all-to-all-start.9 = ((bf16[32,1,12,768]{3,2,1,0:T(8,128)(2,1)}), bf16[32,1,12,768]{3,2,1,0:T(8,128)(2,1)}, u32[]{:S(2)}, u32[]{:S(2)}) async-start(bf16[32,1,12,768]{3,2,1,0:T(8,128)(2,1)} %bitcast.101), calls=%async_computation.9 | async-start | bytes 1572864 | tf_op jit(solution)/shard_map/all_to_all | solution.py:222
  544.7 17.9 %all-to-all-start.5 = ((bf16[2,16,12,768]{3,0,2,1:T(2,128)(2,1)}), bf16[2,16,12,768]{3,0,2,1:T(2,128)(2,1)}, u32[]{:S(2)}, u32[]{:S(2)}) async-start(bf16[2,16,12,768]{3,0,2,1:T(2,128)(2,1)} %bitcast.68), calls=%async_computation.5 | async-start | bytes 1179648 | tf_op jit(solution)/shard_map/all_to_all | solution.py:163
  562.6 15.4 %all-to-all-start.11 = ((bf16[2,16,12,768]{3,0,2,1:T(2,128)(2,1)}), bf16[2,16,12,768]{3,0,2,1:T(2,128)(2,1)}, u32[]{:S(2)}, u32[]{:S(2)}) async-start(bf16[2,16,12,768]{3,0,2,1:T(2,128)(2,1)} %bitcast.610), calls=%async_computation.11 | async-start | bytes 1179648 | tf_op jit(solution)/shard_map/all_to_all | solution.py:236
  567.4 64.8 %all-reduce.34.cloned.1.call-start = ((), (), s32[]{:S(2)}) async-start(), calls=%async_computation.24 | async-start | bytes 1179648 | tf_op jit(solution)/shard_map/psum | solution.py:244
  589.7 98.6 %all-reduce.26.cloned.1.call-start = ((), (), s32[]{:S(2)}) async-start(), calls=%async_computation.20 | async-start | bytes 393216 | tf_op jit(solution)/shard_map/psum | solution.py:265
  693.2 3.3 collective-permute-start.3
  707.3 22.0 %all-to-all-start.12 = ((bf16[32,1,12,768]{3,2,1,0:T(8,128)(2,1)}), bf16[32,1,12,768]{3,2,1,0:T(8,128)(2,1)}, u32[]{:S(2)}, u32[]{:S(2)}) async-start(bf16[32,1,12,768]{3,2,1,0:T(8,128)(2,1)} %bitcast.597), calls=%async_computation.12 | async-start | bytes 1572864 | tf_op jit(solution)/shard_map/all_to_all | solution.py:222
  736.9 15.8 %all-to-all-start.14 = ((bf16[2,16,12,768]{3,0,2,1:T(2,128)(2,1)}), bf16[2,16,12,768]{3,0,2,1:T(2,128)(2,1)}, u32[]{:S(2)}, u32[]{:S(2)}) async-start(bf16[2,16,12,768]{3,0,2,1:T(2,128)(2,1)} %bitcast.612), calls=%async_computation.14 | async-start | bytes 1179648 | tf_op jit(solution)/shard_map/all_to_all | solution.py:236
  741.2 59.4 %all-reduce.28.cloned.1.call-start = ((), (), s32[]{:S(2)}) async-start(), calls=%async_computation.21 | async-start | bytes 393216 | tf_op jit(solution)/shard_map/psum | solution.py:244
  762.4 86.1 %all-reduce.30.cloned.1.call-start = ((), (), s32[]{:S(2)}) async-start(), calls=%async_computation.22 | async-start | bytes 393216 | tf_op jit(solution)/shard_map/psum | solution.py:265
  806.5 133.6 %all-reduce.32.cloned.1.call-start = ((), (), s32[]{:S(2)}) async-start(), calls=%async_computation.23 | async-start | bytes 2359296 | tf_op jit(solution)/shard_map/psum | solution.py:340
  (220 other events, 2775.8 us)
Sparse Core Ops, SparseCore 0:
  16.6 44.6 all-reduce.15
  113.3 39.0 all-reduce.17
  162.0 42.7 all-reduce.19
  310.4 43.6 all-reduce.35
  365.3 42.0 all-reduce.23
  415.9 42.6 all-reduce.21
  589.8 42.4 all-reduce.33
  646.2 42.0 all-reduce.25
  762.5 38.0 all-reduce.27
  806.6 41.8 all-reduce.29
  852.5 87.6 all-reduce.31
where the time goes:
time: 963 us; the launch traced here: 950 us
  waiting for transfers between devices  445 us (46%)
  local copies, waits for them, and re-layouts  132 us (14%)
  matrix products  95.4 us (10%)
  blocking collectives  95.1 us (10%)
  other arithmetic  83 us (9%)
  starting transfers between devices  82.3 us (9%)
  between operations  17 us (2%)
    psum x3, waiting for transfers between devices, layer_forward(): attended = lax.psum(partial_attn, 'head')  117 us
    psum x3, waiting for transfers between devices, layer_backward(): lax.psum(grad_normed_a.astype(jnp.bfloat16), 'head').astype(jnp.float32)  109 us
    psum x3, waiting for transfers between devices, layer_backward(): lax.psum(jnp.sum(grad_slot_rows, axis=1).astype(jnp.bfloat16), 'head')  105 us
    psum x1, blocking collectives, on_device(): lax.psum(table_part.astype(jnp.bfloat16), 'expert').astype(jnp.float32)  75.9 us
    psum x1, waiting for transfers between devices, layer_forward(): lax.psum(slot_part.astype(jnp.bfloat16), 'head').astype(jnp.float32)  38 us
    all_to_all x3, waiting for transfers between devices, layer_backward(): lax.all_to_all(row_buffer, 'expert', split_axis=0, concat_axis=1, tiled=T...  21.8 us
  transfers between devices with their start and end apart: 29, of which 26 were waited for; matrix products, arithmetic and copies ran while one was open for 16% of the time, Pallas kernels for 0%

commit v1 on v0

--- a/solution.py
+++ b/solution.py
@@ -136,7 +136,14 @@
     partial_attn, saved_attn = attend_forward(
         normed_a, proj_weight, out_weight, table, causal, onehot
     )
-    attended = lax.psum(partial_attn, "head")
+    count_all = jax.lax.psum(1, "head")
+    attended = partial_attn
+    for k0 in [
+        [(dev, dev ^ idx) for dev in range(count_all)]
+        for idx in (1, 2, 4, 8, 16)
+        if idx < count_all
+    ]:
+        attended = attended + jax.lax.ppermute(attended, "head", k0)
     middle = values + attended
     scale_m = norm_scale(middle)
     normed_m = (middle * scale_m * gain_m).astype(jnp.bfloat16)

time: 963 us -> 920 us (0.955)
  waiting for transfers between devices: 445 us -> 359 us
  other arithmetic: 83 us -> 101 us
  local copies, waits for them, and re-layouts: 132 us -> 149 us
  starting transfers between devices: 82.3 us -> 92 us
    psum x3 -> x0, waiting for transfers between devices: 117 us -> none  [layer_forward(): attended = lax.psum(partial_attn, 'head')]
    ppermute x0 -> x6, waiting for transfers between devices: none -> 29.4 us  [layer_forward(): attended = attended + jax.lax.ppermute(attended, 'head', k0)]
    ppermute x0 -> x6, starting transfers between devices: none -> 10.5 us  [layer_forward(): attended = attended + jax.lax.ppermute(attended, 'head', k0)]
  transfers between devices with their start and end apart: 29 -> 32, of which waited for: 26 -> 28; matrix products, arithmetic and copies ran while one was open for 16% -> 19% of each run, Pallas kernels for 0% -> 0%
where the time goes in v1:
time: 920 us; the launch traced here: 907 us
  waiting for transfers between devices  359 us (39%)
  local copies, waits for them, and re-layouts  149 us (16%)
  other arithmetic  101 us (11%)
  blocking collectives  97.1 us (11%)
  starting transfers between devices  92 us (10%)
  matrix products  91.2 us (10%)
  between operations  17.4 us (2%)
    psum x3, waiting for transfers between devices, layer_backward(): lax.psum(grad_normed_a.astype(jnp.bfloat16), 'head').astype(jnp.float32)  109 us
    psum x3, waiting for transfers between devices, layer_backward(): lax.psum(jnp.sum(grad_slot_rows, axis=1).astype(jnp.bfloat16), 'head')  106 us
    psum x1, blocking collectives, on_device(): lax.psum(table_part.astype(jnp.bfloat16), 'expert').astype(jnp.float32)  75.9 us
    psum x1, waiting for transfers between devices, layer_forward(): lax.psum(slot_part.astype(jnp.bfloat16), 'head').astype(jnp.float32)  38.2 us
    ppermute x6, waiting for transfers between devices, layer_forward(): attended = attended + jax.lax.ppermute(attended, 'head', k0)  29.4 us
    all_to_all x1, blocking collectives, layer_forward(): lax.all_to_all(buffer.reshape(experts, 1, capacity, width), 'expert', spl...  21.2 us
    all_to_all x3, waiting for transfers between devices, layer_backward(): lax.all_to_all(row_buffer, 'expert', split_axis=0, concat_axis=1, tiled=T...  20.1 us
    all_to_all x3, starting transfers between devices, layer_backward(): lax.all_to_all(row_buffer, 'expert', split_axis=0, concat_axis=1, tiled=T...  18.5 us
  transfers between devices with their start and end apart: 32, of which 28 were waited for; matrix products, arithmetic and copies ran while one was open for 19% of the time, Pallas kernels for 0%

profile of v1, /device:TPU:0, one launch (start us, length us, event | category | flops | bytes accessed | tf_op | source)
XLA Modules:
  0.0 907.3 jit_solution(13211765224380618005)
XLA Ops:
  55.6 21.2 %all_to_all.189 = bf16[32,1,12,768]{3,2,1,0:T(8,128)(2,1)S(1)} all-to-all(bf16[32,1,12,768]{3,2,1,0:T(8,128)(2,1)} %bitcast.589), channel_id=1, replica_groups=mesh['section'=2,'expert'=16,'head'=4] {'expert'}, dimensions={0} | all-to-all | bytes 1179648 | tf_op jit(solution)/shard_map/all_to_all | solution.py:158
  88.1 10.0 %all-to-all-done.1 = bf16[2,16,12,768]{3,0,2,1:T(2,128)(2,1)S(1)} async-done(((bf16[2,16,12,768]{3,0,2,1:T(2,128)(2,1)}), bf16[2,16,12,768]{3,0,2,1:T(2,128)(2,1)S(1)}, u32[]{:S(2)}, u32[]{:S(2)}) %all-to-all-start.1) | async-done | bytes 589856 | tf_op jit(solution)/shard_map/all_to_all | solution.py:170
  106.0 38.2 %all-reduce.13.cloned.1.call-done = bf16[128,2,768]{2,1,0:T(2,128)(2,1)} async-done(((bf16[128,2,768]{2,1,0:T(2,128)(2,1)}), bf16[128,2,768]{2,1,0:T(2,128)(2,1)}) %all-reduce.13.cloned.1.call-update) | async-done | bytes 393232 | tf_op jit(solution)/shard_map/psum | solution.py:178
  153.4 10.9 %collective-permute-done.3 = f32[128,768]{1,0:T(8,128)S(1)} collective-permute-done((f32[128,768]{1,0:T(8,128)S(1)}, f32[128,768]{1,0:T(8,128)S(1)}, u32[]{:S(2)}, u32[]{:S(2)}) %collective-permute-start.3) | collective-permute-done | bytes 393248 | tf_op jit(solution)/shard_map/ppermute | solution.py:146
  166.7 9.8 %collective-permute-done.4 = f32[128,768]{1,0:T(8,128)S(1)} collective-permute-done((f32[128,768]{1,0:T(8,128)S(1)}, f32[128,768]{1,0:T(8,128)S(1)}, u32[]{:S(2)}, u32[]{:S(2)}) %collective-permute-start.4) | collective-permute-done | bytes 393248 | tf_op jit(solution)/shard_map/ppermute | solution.py:146
  184.6 7.0 all-to-all-start.7
  197.8 7.1 all-to-all-done.7
  204.9 4.3 all-to-all-start.2
  215.0 6.6 all-to-all-done.2
  221.6 4.7 all-to-all-start.6
  238.2 6.0 all-to-all-start.3
  255.5 4.8 all-to-all-start.8
  285.8 36.5 %all-reduce.27.cloned.1.call-done = (bf16[128,768]{1,0:T(8,128)(2,1)}, bf16[128,2,768]{2,1,0:T(2,128)(2,1)}) async-done(((bf16[128,768]{1,0:T(8,128)(2,1)}, bf16[128,2,768]{2,1,0:T(2,128)(2,1)}), (bf16[128,768]{1,0:T(8,128)(2,1)}, bf16[128,2,768]{2,1,0:T(2,128)(2,1)})) %all-reduce.27.cloned.1.call-update) | async-done | bytes 589840 | tf_op jit(solution)/shard_map/psum | solution.py:251
  339.5 38.3 %all-reduce.15.cloned.1.call-done = bf16[128,768]{1,0:T(8,128)(2,1)} async-done(((bf16[128,768]{1,0:T(8,128)(2,1)}), bf16[128,768]{1,0:T(8,128)(2,1)}) %all-reduce.15.cloned.1.call-update) | async-done | bytes 196624 | tf_op jit(solution)/shard_map/psum | solution.py:272
  416.6 7.2 all-to-all-start.13
  430.9 4.6 all-to-all-done.13
  447.8 6.9 all-to-all-done.4
  454.6 4.3 all-to-all-start.10
  464.3 8.4 all-to-all-done.10
  472.7 4.7 all-to-all-start.9
  490.2 7.3 all-to-all-start.5
  508.0 4.7 all-to-all-start.11
  539.7 38.6 %all-reduce.25.cloned.1.call-done = (bf16[128,768]{1,0:T(8,128)(2,1)}, bf16[128,2,768]{2,1,0:T(2,128)(2,1)}) async-done(((bf16[128,768]{1,0:T(8,128)(2,1)}, bf16[128,2,768]{2,1,0:T(2,128)(2,1)}), (bf16[128,768]{1,0:T(8,128)(2,1)}, bf16[128,2,768]{2,1,0:T(2,128)(2,1)})) %all-reduce.25.cloned.1.call-update) | async-done | bytes 589840 | tf_op jit(solution)/shard_map/psum | solution.py:251
  599.3 39.0 %all-reduce.17.cloned.1.call-done = bf16[128,768]{1,0:T(8,128)(2,1)} async-done(((bf16[128,768]{1,0:T(8,128)(2,1)}), bf16[128,768]{1,0:T(8,128)(2,1)}) %all-reduce.17.cloned.1.call-update) | async-done | bytes 196624 | tf_op jit(solution)/shard_map/psum | solution.py:272
  663.7 7.2 all-to-all-start.12
  674.2 11.6 %all-to-all-done.12 = bf16[32,1,12,768]{3,2,1,0:T(8,128)(2,1)} async-done(((bf16[32,1,12,768]{3,2,1,0:T(8,128)(2,1)}), bf16[32,1,12,768]{3,2,1,0:T(8,128)(2,1)}, u32[]{:S(2)}, u32[]{:S(2)}) %all-to-all-start.12) | async-done | bytes 589856 | tf_op jit(solution)/shard_map/all_to_all | solution.py:229
  698.1 7.2 add_bitcast_fusion
  719.3 7.2 add_bitcast_fusion.1
  726.5 30.9 %all-reduce.19.cloned.1.call-done = bf16[128,768]{1,0:T(8,128)(2,1)} async-done(((bf16[128,768]{1,0:T(8,128)(2,1)}), bf16[128,768]{1,0:T(8,128)(2,1)}) %all-reduce.19.cloned.1.call-update) | async-done | bytes 196624 | tf_op jit(solution)/shard_map/psum | solution.py:251
  773.2 31.7 %all-reduce.21.cloned.1.call-done = bf16[128,768]{1,0:T(8,128)(2,1)} async-done(((bf16[128,768]{1,0:T(8,128)(2,1)}), bf16[128,768]{1,0:T(8,128)(2,1)}) %all-reduce.21.cloned.1.call-update) | async-done | bytes 196624 | tf_op jit(solution)/shard_map/psum | solution.py:272
  807.3 75.9 %all-reduce = (bf16[1,3,32]{2,1,0:T(4,128)(2,1)}, bf16[1,768]{1,0:T(2,128)(2,1)}, bf16[1,768]{1,0:T(2,128)(2,1)S(1)}, bf16[1,768,32]{1,2,0:T(8,128)(2,1)}) all-reduce(bf16[1,3,32]{2,1,0:T(4,128)(2,1)} %fusion.153, bf16[1,768]{1,0:T(2,128)(2,1)S(1)} %broadcast_in_dim.93, ...), channel_id=1, replica_groups=mesh['section'=2,'expert'=16,'head'=4] {'expert'}, use_global_device_ids=true, to_apply=%region_75.76 | all-reduce | flops 26208 | bytes 104832 | tf_op jit(solution)/shard_map/psum | solution.py:349
  890.4 6.4 all-reduce.23.cloned.1.call-done
  (801 shorter events, 380.8 us)
Async XLA Ops:
  15.3 19.7 %collective-permute-start = (f32[128,768]{1,0:T(8,128)S(1)}, f32[128,768]{1,0:T(8,128)}, u32[]{:S(2)}, u32[]{:S(2)}) collective-permute-start(f32[128,768]{1,0:T(8,128)S(1)} %fusion.272), channel_id=1, source_target_pairs={{0,1},{1,0},{2,3},{3,2},{4,5},{5,4},{6,7},{7,6},{8,9},{9,8},{10,11... | collective-permute-start | bytes 1179656 | tf_op jit(solution)/shard_map/ppermute | solution.py:146
  36.9 12.3 %collective-permute-start.1 = (f32[128,768]{1,0:T(8,128)}, f32[128,768]{1,0:T(8,128)S(1)}, u32[]{:S(2)}, u32[]{:S(2)}) collective-permute-start(f32[128,768]{1,0:T(8,128)} %add.454), channel_id=1, source_target_pairs={{0,2},{1,3},{2,0},{3,1},{4,6},{5,7},{6,4},{7,5},{8,10},{9,11},{10,... | collective-permute-start | bytes 1179656 | tf_op jit(solution)/shard_map/ppermute | solution.py:146
  84.1 14.0 %all-to-all-start.1 = ((bf16[2,16,12,768]{3,0,2,1:T(2,128)(2,1)}), bf16[2,16,12,768]{3,0,2,1:T(2,128)(2,1)S(1)}, u32[]{:S(2)}, u32[]{:S(2)}) async-start(bf16[2,16,12,768]{3,0,2,1:T(2,128)(2,1)} %bitcast.602), calls=%async_computation.1 | async-start | bytes 1179648 | tf_op jit(solution)/shard_map/all_to_all | solution.py:170
  87.7 56.6 %all-reduce.13.cloned.1.call-start = ((), (), s32[]{:S(2)}) async-start(), calls=%async_computation.15 | async-start | bytes 786432 | tf_op jit(solution)/shard_map/psum | solution.py:178
  147.5 2.5 collective-permute-start.2
  152.8 11.5 %collective-permute-start.3 = (f32[128,768]{1,0:T(8,128)S(1)}, f32[128,768]{1,0:T(8,128)S(1)}, u32[]{:S(2)}, u32[]{:S(2)}) collective-permute-start(f32[128,768]{1,0:T(8,128)S(1)} %fusion.270), channel_id=1, source_target_pairs={{0,1},{1,0},{2,3},{3,2},{4,5},{5,4},{6,7},{7,6},{8,9},{9,8},{10,11... | collective-permute-start | bytes 1179656 | tf_op jit(solution)/shard_map/ppermute | solution.py:146
  164.3 12.2 %collective-permute-start.4 = (f32[128,768]{1,0:T(8,128)S(1)}, f32[128,768]{1,0:T(8,128)S(1)}, u32[]{:S(2)}, u32[]{:S(2)}) collective-permute-start(f32[128,768]{1,0:T(8,128)S(1)} %add.465), channel_id=1, source_target_pairs={{0,2},{1,3},{2,0},{3,1},{4,6},{5,7},{6,4},{7,5},{8,10},{9,11},{10,... | collective-permute-start | bytes 1179656 | tf_op jit(solution)/shard_map/ppermute | solution.py:146
  184.6 20.3 %all-to-all-start.7 = ((bf16[32,1,12,768]{3,2,1,0:T(8,128)(2,1)}), bf16[32,1,12,768]{3,2,1,0:T(8,128)(2,1)}, u32[]{:S(2)}, u32[]{:S(2)}) async-start(bf16[32,1,12,768]{3,2,1,0:T(8,128)(2,1)} %bitcast.587), calls=%async_computation.7 | async-start | bytes 1572864 | tf_op jit(solution)/shard_map/all_to_all | solution.py:230
  204.9 16.7 %all-to-all-start.2 = ((bf16[32,1,12,768]{3,2,1,0:T(8,128)(2,1)}), bf16[32,1,12,768]{3,2,1,0:T(8,128)(2,1)}, u32[]{:S(2)}, u32[]{:S(2)}) async-start(bf16[32,1,12,768]{3,2,1,0:T(8,128)(2,1)} %bitcast.585), calls=%async_computation.2 | async-start | bytes 1572864 | tf_op jit(solution)/shard_map/all_to_all | solution.py:158
  221.6 16.6 %all-to-all-start.6 = ((bf16[32,1,12,768]{3,2,1,0:T(8,128)(2,1)}), bf16[32,1,12,768]{3,2,1,0:T(8,128)(2,1)}, u32[]{:S(2)}, u32[]{:S(2)}) async-start(bf16[32,1,12,768]{3,2,1,0:T(8,128)(2,1)} %bitcast.80), calls=%async_computation.6 | async-start | bytes 1572864 | tf_op jit(solution)/shard_map/all_to_all | solution.py:229
  238.2 16.5 %all-to-all-start.3 = ((bf16[2,16,12,768]{3,0,2,1:T(2,128)(2,1)}), bf16[2,16,12,768]{3,0,2,1:T(2,128)(2,1)S(1)}, u32[]{:S(2)}, u32[]{:S(2)}) async-start(bf16[2,16,12,768]{3,0,2,1:T(2,128)(2,1)} %bitcast.600), calls=%async_computation.3 | async-start | bytes 1179648 | tf_op jit(solution)/shard_map/all_to_all | solution.py:170
  255.5 15.3 %all-to-all-start.8 = ((bf16[2,16,12,768]{3,0,2,1:T(2,128)(2,1)}), bf16[2,16,12,768]{3,0,2,1:T(2,128)(2,1)S(1)}, u32[]{:S(2)}, u32[]{:S(2)}) async-start(bf16[2,16,12,768]{3,0,2,1:T(2,128)(2,1)} %bitcast.88), calls=%async_computation.8 | async-start | bytes 1179648 | tf_op jit(solution)/shard_map/all_to_all | solution.py:243
  260.3 62.0 %all-reduce.27.cloned.1.call-start = ((), (), s32[]{:S(2)}) async-start(), calls=%async_computation.22 | async-start | bytes 1179648 | tf_op jit(solution)/shard_map/psum | solution.py:251
  279.4 98.4 %all-reduce.15.cloned.1.call-start = ((), (), s32[]{:S(2)}) async-start(), calls=%async_computation.16 | async-start | bytes 393216 | tf_op jit(solution)/shard_map/psum | solution.py:272
  337.5 42.2 %collective-permute-start.5 = (bf16[128,768]{1,0:T(8,128)(2,1)}, bf16[128,768]{1,0:T(8,128)(2,1)}, u32[]{:S(2)}, u32[]{:S(2)}) collective-permute-start(bf16[128,768]{1,0:T(8,128)(2,1)} %get-tuple-element.84), channel_id=1, source_target_pairs={{0,64},{1,65},{2,66},{3,67},{4,68},{5,69},{6,70},{7,71},{8,72},{9,... | collective-permute-start | bytes 589832 | tf_op jit(solution)/shard_map/ppermute | solution.py:14
  385.2 8.9 collective-permute-start.6
  394.1 9.8 %collective-permute-start.7 = (f32[128,768]{1,0:T(8,128)S(1)}, f32[128,768]{1,0:T(8,128)}, u32[]{:S(2)}, u32[]{:S(2)}) collective-permute-start(f32[128,768]{1,0:T(8,128)S(1)} %add.476), channel_id=1, source_target_pairs={{0,2},{1,3},{2,0},{3,1},{4,6},{5,7},{6,4},{7,5},{8,10},{9,11},{10,... | collective-permute-start | bytes 1179656 | tf_op jit(solution)/shard_map/ppermute | solution.py:146
  416.6 18.8 %all-to-all-start.13 = ((bf16[32,1,12,768]{3,2,1,0:T(8,128)(2,1)}), bf16[32,1,12,768]{3,2,1,0:T(8,128)(2,1)}, u32[]{:S(2)}, u32[]{:S(2)}) async-start(bf16[32,1,12,768]{3,2,1,0:T(8,128)(2,1)} %bitcast.129), calls=%async_computation.13 | async-start | bytes 1572864 | tf_op jit(solution)/shard_map/all_to_all | solution.py:230
  425.9 15.2 %collective-permute-start.8 = (bf16[128,768]{1,0:T(8,128)(2,1)}, bf16[128,768]{1,0:T(8,128)(2,1)}, u32[]{:S(2)}, u32[]{:S(2)}) collective-permute-start(bf16[128,768]{1,0:T(8,128)(2,1)} %get-tuple-element.105), channel_id=1, source_target_pairs={{64,0},{65,1},{66,2},{67,3},{68,4},{69,5},{70,6},{71,7},{72,8},{73... | collective-permute-start | bytes 589832 | tf_op jit(solution)/shard_map/ppermute | solution.py:14
  435.5 19.2 %all-to-all-start.4 = ((bf16[32,1,12,768]{3,2,1,0:T(8,128)(2,1)}), bf16[32,1,12,768]{3,2,1,0:T(8,128)(2,1)}, u32[]{:S(2)}, u32[]{:S(2)}) async-start(bf16[32,1,12,768]{3,2,1,0:T(8,128)(2,1)} %bitcast.584), calls=%async_computation.4 | async-start | bytes 1572864 | tf_op jit(solution)/shard_map/all_to_all | solution.py:158
  454.6 18.0 %all-to-all-start.10 = ((bf16[32,1,12,768]{3,2,1,0:T(8,128)(2,1)}), bf16[32,1,12,768]{3,2,1,0:T(8,128)(2,1)}, u32[]{:S(2)}, u32[]{:S(2)}) async-start(bf16[32,1,12,768]{3,2,1,0:T(8,128)(2,1)} %bitcast.583), calls=%async_computation.10 | async-start | bytes 1572864 | tf_op jit(solution)/shard_map/all_to_all | solution.py:230
  472.7 17.5 %all-to-all-start.9 = ((bf16[32,1,12,768]{3,2,1,0:T(8,128)(2,1)}), bf16[32,1,12,768]{3,2,1,0:T(8,128)(2,1)}, u32[]{:S(2)}, u32[]{:S(2)}) async-start(bf16[32,1,12,768]{3,2,1,0:T(8,128)(2,1)} %bitcast.101), calls=%async_computation.9 | async-start | bytes 1572864 | tf_op jit(solution)/shard_map/all_to_all | solution.py:229
  490.2 17.8 %all-to-all-start.5 = ((bf16[2,16,12,768]{3,0,2,1:T(2,128)(2,1)}), bf16[2,16,12,768]{3,0,2,1:T(2,128)(2,1)}, u32[]{:S(2)}, u32[]{:S(2)}) async-start(bf16[2,16,12,768]{3,0,2,1:T(2,128)(2,1)} %bitcast.68), calls=%async_computation.5 | async-start | bytes 1179648 | tf_op jit(solution)/shard_map/all_to_all | solution.py:170
  508.0 15.2 %all-to-all-start.11 = ((bf16[2,16,12,768]{3,0,2,1:T(2,128)(2,1)}), bf16[2,16,12,768]{3,0,2,1:T(2,128)(2,1)}, u32[]{:S(2)}, u32[]{:S(2)}) async-start(bf16[2,16,12,768]{3,0,2,1:T(2,128)(2,1)} %bitcast.599), calls=%async_computation.11 | async-start | bytes 1179648 | tf_op jit(solution)/shard_map/all_to_all | solution.py:243
  512.7 65.7 %all-reduce.25.cloned.1.call-start = ((), (), s32[]{:S(2)}) async-start(), calls=%async_computation.21 | async-start | bytes 1179648 | tf_op jit(solution)/shard_map/psum | solution.py:251
  535.0 103.3 %all-reduce.17.cloned.1.call-start = ((), (), s32[]{:S(2)}) async-start(), calls=%async_computation.17 | async-start | bytes 393216 | tf_op jit(solution)/shard_map/psum | solution.py:272
  643.4 3.3 collective-permute-start.9
  663.7 22.2 %all-to-all-start.12 = ((bf16[32,1,12,768]{3,2,1,0:T(8,128)(2,1)}), bf16[32,1,12,768]{3,2,1,0:T(8,128)(2,1)}, u32[]{:S(2)}, u32[]{:S(2)}) async-start(bf16[32,1,12,768]{3,2,1,0:T(8,128)(2,1)} %bitcast.586), calls=%async_computation.12 | async-start | bytes 1572864 | tf_op jit(solution)/shard_map/all_to_all | solution.py:229
  693.6 16.0 %all-to-all-start.14 = ((bf16[2,16,12,768]{3,0,2,1:T(2,128)(2,1)}), bf16[2,16,12,768]{3,0,2,1:T(2,128)(2,1)}, u32[]{:S(2)}, u32[]{:S(2)}) async-start(bf16[2,16,12,768]{3,0,2,1:T(2,128)(2,1)} %bitcast.601), calls=%async_computation.14 | async-start | bytes 1179648 | tf_op jit(solution)/shard_map/all_to_all | solution.py:243
  697.8 59.6 %all-reduce.19.cloned.1.call-start = ((), (), s32[]{:S(2)}) async-start(), calls=%async_computation.18 | async-start | bytes 393216 | tf_op jit(solution)/shard_map/psum | solution.py:251
  719.3 85.6 %all-reduce.21.cloned.1.call-start = ((), (), s32[]{:S(2)}) async-start(), calls=%async_computation.19 | async-start | bytes 393216 | tf_op jit(solution)/shard_map/psum | solution.py:272
  762.9 133.9 %all-reduce.23.cloned.1.call-start = ((), (), s32[]{:S(2)}) async-start(), calls=%async_computation.20 | async-start | bytes 2359296 | tf_op jit(solution)/shard_map/psum | solution.py:347
  (224 other events, 2130.2 us)
Sparse Core Ops, SparseCore 0:
  104.7 39.4 all-reduce.12
  279.5 42.7 all-reduce.26
  335.6 42.0 all-reduce.14
  535.1 43.2 all-reduce.24
  596.2 42.0 all-reduce.16
  719.3 38.0 all-reduce.18
  763.0 41.8 all-reduce.20
  809.2 87.5 all-reduce.22
